TPU v7x, 256 devices: a whole 4x4x8 slice. The times are simulated.
256 devices in a mesh: chan: 64 (over z, y, core), row: 4 (over x).
Axes of the slice: x: 4, y: 4, z: 8, core: 2. Of those that a mesh axis runs over, the one named last changes fastest.
Arguments:
- generator: float32 [64, 1280, 1280], P('chan', 'row'), as said below
- hamiltonian: float32 [64, 1280, 1280], P('chan', 'row'), as said below
- recoupling: float32 [64, 1280, 1280], P('chan')
- channel_size: int32 [64], P('chan'), may hold values from 128 to 1280, as said below
- hole_first: int32 [64, 1280], P('chan'), may hold values 0 or 1
- hole_second: int32 [64, 1280], P('chan'), may hold values 0 or 1
Outputs:
- derivative: float32 [64, 1280, 1280], P('chan', 'row')
Inputs may be any that keep to these rules, and one draw needn't show every extreme that they name: generator is antisymmetric and hamiltonian symmetric in every channel block. hamiltonian is symmetric in every channel block. `channel_size`: some channel has exactly 1280 states.
All inputs are finite; a program needn't handle non-finite values. No bound on the sum of `hole_first` or of `hole_second` on one device may be relied on, other than what follows from the above.
Results may differ from a plain program's by a relative error of at most 0.000076.
Values sent between devices are 32-bit elements; how exact they have to be, the bound alone decides.
No kernel may reach another device: no remote copies, remote signals or barrier semaphores. Data moves between devices by JAX's collectives and lax.ppermute only.
A program may use at most 128 MiB of HBM per device.

v0:
```python
import jax
import jax.numpy as jnp
from jax import lax
from jax.sharding import PartitionSpec as P


def batched(left, right):
    return jnp.einsum("cij,cjk->cik", left, right, precision=lax.Precision.HIGHEST)


def shards(generator, hamiltonian, recoupling, channel_size, hole_first, hole_second):
    local_count = generator.shape[0]
    row_count = generator.shape[1]
    block_order = generator.shape[2]
    chan_count = lax.axis_size("chan")
    row_index = lax.axis_index("row")
    positions = jnp.arange(block_order, dtype=jnp.int32)
    inside = (positions[None, :] < channel_size[:, None]).astype(jnp.float32)
    row_inside = lax.dynamic_slice_in_dim(inside, row_index * row_count, row_count, 1)
    block_mask = row_inside[:, :, None] * inside[:, None, :]
    gen_live = generator * block_mask
    ham_live = hamiltonian * block_mask
    weight_pp = (1 - hole_first - hole_second).astype(jnp.float32)
    weight_ph = (hole_first - hole_second).astype(jnp.float32)
    piece_shape = (local_count, row_count, chan_count, block_order // chan_count)
    gen_moved, ham_moved = (
        lax.all_to_all(
            gen_live.reshape(piece_shape), "chan", split_axis=2, concat_axis=2, tiled=True
        ),
        lax.all_to_all(
            ham_live.reshape(piece_shape), "chan", split_axis=2, concat_axis=2, tiled=True
        ),
    )
    gen_bar = batched(gen_moved.reshape(generator.shape), recoupling)
    ham_bar = batched(ham_moved.reshape(generator.shape), recoupling)
    pieces = (
        lax.all_gather(gen_bar, "row", axis=1, tiled=True),
        lax.all_gather(ham_bar, "row", axis=1, tiled=True),
    )
    factor = weight_ph[:, None, :]
    gen_cols = gen_bar * factor
    ham_cols = ham_bar * factor
    ph_term = batched(gen_cols, pieces[1]) - batched(ham_cols, pieces[0])
    turned = jnp.einsum("cij,ckj->cik", ph_term, recoupling, precision=lax.Precision.HIGHEST)
    back_moved = lax.all_to_all(
        turned.reshape(piece_shape), "chan", split_axis=2, concat_axis=2, tiled=True
    )
    ph_back = back_moved.reshape(generator.shape)
    pieces = (
        lax.all_gather(gen_live, "row", axis=1, tiled=True),
        lax.all_gather(ham_live, "row", axis=1, tiled=True),
    )
    factor = weight_pp[:, None, :]
    gen_cols = gen_live * factor
    ham_cols = ham_live * factor
    ladder = batched(gen_cols, pieces[1]) - batched(ham_cols, pieces[0])
    return (ladder + ph_back) * block_mask


def solution(mesh):
    in_specs = (
        P("chan", "row", None),
        P("chan", "row", None),
        P("chan", None, None),
        P("chan"),
        P("chan", None),
        P("chan", None),
    )
    out_specs = P("chan", "row", None)
    return jax.shard_map(shards, mesh=mesh, in_specs=in_specs, out_specs=out_specs, check_vma=False)
```

profile of v0, /device:TPU:1, one launch (start us, length us, event | category | flops | bytes accessed | tf_op | source)
XLA Modules:
  0.0 404.9 jit_solution(18243573594442668754)
XLA Ops:
  6.5 0.0 all-gather.11.cloned.1.call-start
  7.2 2.2 multiply_multiply_fusion.1
  9.4 0.0 copy-start.1
  9.5 0.0 copy-start.5
  9.5 3.6 copy.20
  13.0 0.0 copy-done.1
  13.0 60.2 %all_to_all.15 = f32[1,320,64,20]{1,0,3,2:T(1,128)} all-to-all(f32[1,320,64,20]{1,0,3,2:T(1,128)} %bitcast.47), channel_id=1, replica_groups=mesh['chan'=64,'row'=4] {'chan'}, dimensions={2} | all-to-all | bytes 3276800 | tf_op jit(solution)/shard_map/all_to_all | solution.py:30
  73.2 7.7 %reduce.4 = f32[320,64,20]{0,2,1:T(8,128)} reduce(f32[1,320,64,20]{1,0,3,2:T(1,128)} %all_to_all.15, f32[]{:T(128)} %constant.18), dimensions={0}, to_apply=%all_to_all.10.reduce_sub_computation | reduce | bytes 3276804 | tf_op jit(solution)/shard_map/all_to_all | solution.py:30
  81.0 2.9 reshape.159
  83.8 11.5 %fusion = f32[320,1280]{1,0:T(8,128)} fusion(f32[320,1280]{0,1:T(8,128)} %reshape.159, f32[1,1280,1280]{2,1,0:T(8,128)} %param.8), kind=kOutput, calls=%fused_computation | convolution fusion | flops 6291456000 | bytes 9830400 | tf_op jit(solution)/shard_map/cij,cjk->cik/dot_general | solution.py:8
  95.3 0.0 all-gather.11.cloned.1.call-update
  95.3 0.0 all-gather.13.cloned.1.call-start
  95.4 0.0 copy-done.5
  95.4 3.2 copy.19
  98.6 54.1 %all_to_all.16 = f32[1,320,64,20]{1,0,3,2:T(1,128)S(1)} all-to-all(f32[1,320,64,20]{1,0,3,2:T(1,128)} %bitcast.48), channel_id=1, replica_groups=mesh['chan'=64,'row'=4] {'chan'}, dimensions={2} | all-to-all | bytes 3276800 | tf_op jit(solution)/shard_map/all_to_all | solution.py:27
  152.6 7.0 %reduce.2 = f32[320,64,20]{0,2,1:T(8,128)} reduce(f32[1,320,64,20]{1,0,3,2:T(1,128)S(1)} %all_to_all.16, f32[]{:T(128)} %constant.18), dimensions={0}, to_apply=%all_to_all.9.reduce_sub_computation | reduce | bytes 3276804 | tf_op jit(solution)/shard_map/all_to_all | solution.py:27
  159.6 2.0 reshape.156
  161.6 10.9 %fusion.2 = f32[320,1280]{1,0:T(8,128)} fusion(f32[320,1280]{0,1:T(8,128)S(1)} %reshape.156, f32[1,1280,1280]{2,1,0:T(8,128)} %param.8), kind=kOutput, calls=%fused_computation.2 | convolution fusion | flops 6291456000 | bytes 9830400 | tf_op jit(solution)/shard_map/cij,cjk->cik/dot_general | solution.py:8
  172.5 0.0 all-gather.13.cloned.1.call-update
  172.5 0.0 all-gather.9.cloned.1.call-start
  172.5 0.7 all-gather.9.cloned.1.call-update
  173.2 0.0 all-gather.7.cloned.1.call-start
  173.3 0.5 all-gather.7.cloned.1.call-update
  173.8 0.0 copy-start.7
  173.8 0.0 copy-start.8
  173.8 0.0 copy-start.4
  173.8 8.4 %dot_general.37 = f32[64,20,1280]{2,1,0:T(8,128)} reshape(f32[1,1280,1280]{2,1,0:T(8,128)} %param.8) | data formatting | bytes 13107200 | tf_op jit(solution)/shard_map/cij,ckj->cik/dot_general | solution.py:44
  182.3 0.0 copy-done.7
  182.3 0.0 copy-done.8
  182.3 0.0 all-gather.11.cloned.1.call-done
  182.4 0.0 copy-done.4
  182.4 0.0 copy-start.3
  182.4 11.7 %fusion.26 = f32[320,1280]{1,0:T(8,128)} fusion(f32[1280,1280]{1,0:T(8,128)} %all-gather.11.cloned.1.call-done, f32[320,1280]{1,0:T(8,128)S(1)} %copy-done.4, f32[1280]{0:T(1024)S(1)} %get-tuple-element.6), kind=kOutput, calls=%fused_computation.21 | convolution fusion | flops 6291865600 | bytes 9835520 | tf_op jit(solution)/shard_map/cij,cjk->cik/dot_general | solution.py:8
  194.0 46.6 %all-gather.13.cloned.1.call-done = f32[1280,1280]{1,0:T(8,128)} async-done(((f32[320,1280]{1,0:T(8,128)}), f32[1280,1280]{1,0:T(8,128)}) %all-gather.13.cloned.1.call-update) | async-done | bytes 6553616 | tf_op jit(solution)/shard_map/all_gather | solution.py:37
  240.6 0.0 copy-done.3
  240.6 10.5 %fusion.19 = f32[320,1280,1]{1,0,2:T(8,128)S(1)} fusion(f32[320,1280]{1,0:T(8,128)} %fusion.26, f32[1280,1280]{1,0:T(8,128)} %all-gather.13.cloned.1.call-done, f32[320,1280]{1,0:T(8,128)S(1)} %copy-done.3, f32[1280]{0:T(1024)S(1)} %get-tuple-element.6), kind=kOutput, calls=%fused_computation.14 | convolution fusion | flops 6292275200 | bytes 11473920 | tf_op jit(solution)/shard_map/cij,cjk->cik/dot_general | solution.py:8
  251.2 0.0 copy-done
  251.2 11.5 %fusion.30 = f32[1,320,64,20]{1,2,3,0:T(8,128)S(1)} fusion(f32[320,1280,1]{1,0,2:T(8,128)S(1)} %fusion.19, f32[64,20,1280]{2,1,0:T(8,128)S(1)} %copy-done), kind=kOutput, calls=%fused_computation.25 | convolution fusion | flops 6291456000 | bytes 9830400 | tf_op jit(solution)/shard_map/cij,ckj->cik/dot_general | solution.py:44
  262.7 3.3 copy.22
  266.0 11.0 %all-to-all-start.2 = ((f32[1,320,64,20]{1,0,3,2:T(1,128)}), f32[1,320,64,20]{1,0,3,2:T(1,128)}, u32[]{:S(2)}, u32[]{:S(2)}) async-start(f32[1,320,64,20]{1,0,3,2:T(1,128)} %copy.22), calls=%async_computation.2 | async-start | bytes 3932160 | tf_op jit(solution)/shard_map/all_to_all | solution.py:45
  277.0 36.6 %all-gather.9.cloned.1.call-done = f32[1,1280,1280]{2,1,0:T(8,128)} async-done(((f32[1,320,1280]{2,1,0:T(8,128)}), f32[1,1280,1280]{2,1,0:T(8,128)}) %all-gather.9.cloned.1.call-update) | async-done | bytes 6553616 | tf_op jit(solution)/shard_map/all_gather | solution.py:50
  313.6 10.9 %fusion.4 = f32[320,1280]{1,0:T(8,128)} fusion(f32[1,1280,1280]{2,1,0:T(8,128)} %all-gather.9.cloned.1.call-done, f32[1,320,1280]{2,1,0:T(8,128)S(1)} %copy-done.2, f32[1280]{0:T(1024)S(1)} %get-tuple-element.5), kind=kOutput, calls=%fused_computation.4 | convolution fusion | flops 6291865600 | bytes 9835520 | tf_op jit(solution)/shard_map/cij,cjk->cik/dot_general | solution.py:8
  324.5 0.0 all-to-all-done.2
  324.5 6.3 %reduce.5 = f32[320,64,20]{0,2,1:T(8,128)S(1)} reduce(f32[1,320,64,20]{1,0,3,2:T(1,128)} %all-to-all-done.2, f32[]{:T(128)} %constant.18), dimensions={0}, to_apply=%all_to_all.11.reduce_sub_computation | reduce | bytes 3276804 | tf_op jit(solution)/shard_map/all_to_all | solution.py:45
  330.8 1.5 reshape.162
  332.3 2.3 copy.23
  334.6 51.8 %all-gather.7.cloned.1.call-done = f32[1,1280,1280]{2,1,0:T(8,128)} async-done(((f32[1,320,1280]{2,1,0:T(8,128)}), f32[1,1280,1280]{2,1,0:T(8,128)}) %all-gather.7.cloned.1.call-update) | async-done | bytes 6553616 | tf_op jit(solution)/shard_map/all_gather | solution.py:51
  386.4 11.5 %fusion.20 = f32[1,320,1280]{2,1,0:T(8,128)} fusion(f32[320,1280]{1,0:T(8,128)S(1)} %copy.23, f32[320,1280]{1,0:T(8,128)} %fusion.4, f32[1,1280,1280]{2,1,0:T(8,128)} %all-gather.7.cloned.1.call-done, f32[1280]{0:T(1024)S(1)} %fusion.37, f32[320]{0:T(512)S(1)} %fusion.38, f32[1280]{0:T(1024)S(1)} %get-tuple-element.5, f32[1,320,1280]{2,1,0:T(8,128)S(1)} %copy-done.6), kind=kOutput, calls=%fused_computation.15 | convolution fusion | flops 6294323200 | bytes 13118720 | tf_op jit(solution)/shard_map/cij,cjk->cik/dot_general | solution.py:8
  (8 shorter events, 0.1 us)
Async XLA Ops:
  6.5 175.8 %all-gather.11.cloned.1.call-start = ((), (), s32[]{:S(2)}) async-start(), calls=%async_computation.5 | async-start | bytes 8192000 | tf_op jit(solution)/shard_map/all_gather | solution.py:38
  9.4 3.6 copy-start.1
  9.5 85.9 %copy-start.5 = (f32[1,320,1280]{2,1,0:T(8,128)}, f32[1,320,1280]{2,1,0:T(8,128)S(1)}, u32[]{:S(2)}) copy-start(f32[1,320,1280]{2,1,0:T(8,128)S(1)} %get-tuple-element.7) | copy-start | bytes 4915204
  95.3 145.3 %all-gather.13.cloned.1.call-start = ((), (), s32[]{:S(2)}) async-start(), calls=%async_computation.6 | async-start | bytes 8192000 | tf_op jit(solution)/shard_map/all_gather | solution.py:37
  172.5 141.1 %all-gather.9.cloned.1.call-start = ((), (), s32[]{:S(2)}) async-start(), calls=%async_computation.4 | async-start | bytes 8192000 | tf_op jit(solution)/shard_map/all_gather | solution.py:50
  173.2 213.2 %all-gather.7.cloned.1.call-start = ((), (), s32[]{:S(2)}) async-start(), calls=%async_computation.3 | async-start | bytes 8192000 | tf_op jit(solution)/shard_map/all_gather | solution.py:51
  173.8 8.5 %copy-start.7 = (s32[1,1280]{1,0:T(1,128)S(1)}, s32[1,1280]{1,0:T(1,128)}, u32[]{:S(2)}) copy-start(s32[1,1280]{1,0:T(1,128)} %param.11) | copy-start | bytes 15364
  173.8 8.5 %copy-start.8 = (s32[1,1280]{1,0:T(1,128)S(1)}, s32[1,1280]{1,0:T(1,128)}, u32[]{:S(2)}) copy-start(s32[1,1280]{1,0:T(1,128)} %param.10) | copy-start | bytes 15364
  173.8 8.5 %copy-start.4 = (f32[320,1280]{1,0:T(8,128)S(1)}, f32[320,1280]{1,0:T(8,128)}, u32[]{:S(2)}) copy-start(f32[320,1280]{1,0:T(8,128)} %fusion.2) | copy-start | bytes 4915204
  182.4 58.2 %copy-start.3 = (f32[320,1280]{1,0:T(8,128)S(1)}, f32[320,1280]{1,0:T(8,128)}, u32[]{:S(2)}) copy-start(f32[320,1280]{1,0:T(8,128)} %fusion) | copy-start | bytes 4915204
  240.6 10.5 %copy-start = (f32[64,20,1280]{2,1,0:T(8,128)S(1)}, f32[64,20,1280]{2,1,0:T(8,128)}, u32[]{:S(2)}) copy-start(f32[64,20,1280]{2,1,0:T(8,128)} %dot_general.37) | copy-start | bytes 19660804
  266.0 47.6 %copy-start.2 = (f32[1,320,1280]{2,1,0:T(8,128)S(1)}, f32[1,320,1280]{2,1,0:T(8,128)}, u32[]{:S(2)}) copy-start(f32[1,320,1280]{2,1,0:T(8,128)} %copy-done.1) | copy-start | bytes 4915204
  266.0 58.5 %all-to-all-start.2 = ((f32[1,320,64,20]{1,0,3,2:T(1,128)}), f32[1,320,64,20]{1,0,3,2:T(1,128)}, u32[]{:S(2)}, u32[]{:S(2)}) async-start(f32[1,320,64,20]{1,0,3,2:T(1,128)} %copy.22), calls=%async_computation.2 | async-start | bytes 3932160 | tf_op jit(solution)/shard_map/all_to_all | solution.py:45
  332.3 54.2 %copy-start.6 = (f32[1,320,1280]{2,1,0:T(8,128)S(1)}, f32[1,320,1280]{2,1,0:T(8,128)}, u32[]{:S(2)}) copy-start(f32[1,320,1280]{2,1,0:T(8,128)} %param.6) | copy-start | bytes 4915204
Sparse Core Ops, SparseCore 0:
  95.4 67.9 all-gather.10
  172.6 67.9 all-gather.12
  242.4 71.1 all-gather.8
  315.3 71.1 all-gather.6
where the time goes:
time: 411 us; the launch traced here: 405 us
  waiting for transfers between devices  136 us (33%)
  blocking collectives  114 us (28%)
  matrix products  78.5 us (19%)
  local copies, waits for them, and re-layouts  27.1 us (7%)
  other arithmetic  23.3 us (6%)
  between operations  14.4 us (4%)
  starting transfers between devices  11.2 us (3%)
    dot_general x6, matrix products, batched(): jnp.einsum('cij,cjk->cik', left, right, precision=lax.Precision.HIGHEST)  66.9 us
    all_to_all x1, blocking collectives, shards(): lax.all_to_all(ham_live.reshape(piece_shape), 'chan', split_axis=2, conca...  60.2 us
    all_to_all x1, blocking collectives, shards(): lax.all_to_all(gen_live.reshape(piece_shape), 'chan', split_axis=2, conca...  54.1 us
    all_gather x1, waiting for transfers between devices, shards(): lax.all_gather(ham_live, 'row', axis=1, tiled=True)  51.8 us
    all_gather x1, waiting for transfers between devices, shards(): lax.all_gather(gen_bar, 'row', axis=1, tiled=True)  46.6 us
    all_gather x1, waiting for transfers between devices, shards(): lax.all_gather(gen_live, 'row', axis=1, tiled=True)  36.6 us
    dot_general x2, local copies, waits for them, and re-layouts, shards(): jnp.einsum('cij,ckj->cik', ph_term, recoupling, precision=lax.Precision.H...  11.7 us
    dot_general x1, matrix products, shards(): jnp.einsum('cij,ckj->cik', ph_term, recoupling, precision=lax.Precision.H...  11.5 us
  transfers between devices with their start and end apart: 5, of which 3 were waited for; matrix products, arithmetic and copies ran while one was open for 22% of the time, Pallas kernels for 0%

commit v1 on v0

--- a/solution.py
+++ b/solution.py
@@ -27,8 +27,14 @@
         lax.all_to_all(
             gen_live.reshape(piece_shape), "chan", split_axis=2, concat_axis=2, tiled=True
         ),
-        lax.all_to_all(
-            ham_live.reshape(piece_shape), "chan", split_axis=2, concat_axis=2, tiled=True
+        jnp.concatenate(
+            lax.all_to_all(
+                jnp.stack(jnp.split(ham_live.reshape(piece_shape), lax.axis_size("chan"), axis=2)),
+                "chan",
+                0,
+                0,
+            ),
+            axis=2,
         ),
     )
     gen_bar = batched(gen_moved.reshape(generator.shape), recoupling)

time: 411 us -> 435 us (1.058)
  local copies, waits for them, and re-layouts: 27.1 us -> 48 us
  blocking collectives: 114 us -> 124 us
  other arithmetic: 23.3 us -> 17.8 us
    another operation x2 -> x8, local copies, waits for them, and re-layouts: 4.85 us -> 24.5 us  [the longest x6 18.9 us: shards(): jnp.stack(jnp.split(ham_live.reshape(piece_shape), lax.axis_size('chan'),...]
    all_to_all x1, blocking collectives: 60.2 us -> 71.3 us  [shards(): lax.all_to_all(jnp.stack(jnp.split(ham_live.reshape(piece_shape), lax.axi...]
    all_to_all x1 -> x0, other arithmetic: 7.73 us -> none  [shards(): lax.all_to_all(ham_live.reshape(piece_shape), 'chan', split_axis=2, conca...]
where the time goes in v1:
time: 435 us; the launch traced here: 428 us
  waiting for transfers between devices  133 us (31%)
  blocking collectives  124 us (29%)
  matrix products  79 us (18%)
  local copies, waits for them, and re-layouts  48 us (11%)
  other arithmetic  17.8 us (4%)
  between operations  14.4 us (3%)
  starting transfers between devices  11.2 us (3%)
    all_to_all x1, blocking collectives, shards(): lax.all_to_all(jnp.stack(jnp.split(ham_live.reshape(piece_shape), lax.axi...  71.3 us
    dot_general x6, matrix products, batched(): jnp.einsum('cij,cjk->cik', left, right, precision=lax.Precision.HIGHEST)  67.5 us
    all_to_all x1, blocking collectives, shards(): lax.all_to_all(gen_live.reshape(piece_shape), 'chan', split_axis=2, conca...  52.5 us
    all_gather x1, waiting for transfers between devices, shards(): lax.all_gather(ham_live, 'row', axis=1, tiled=True)  49.1 us
    all_gather x1, waiting for transfers between devices, shards(): lax.all_gather(gen_bar, 'row', axis=1, tiled=True)  46.5 us
    all_gather x1, waiting for transfers between devices, shards(): lax.all_gather(gen_live, 'row', axis=1, tiled=True)  36.5 us
    another operation x6, local copies, waits for them, and re-layouts, shards(): jnp.stack(jnp.split(ham_live.reshape(piece_shape), lax.axis_size('chan'),...  18.9 us
    dot_general x2, local copies, waits for them, and re-layouts, shards(): jnp.einsum('cij,ckj->cik', ph_term, recoupling, precision=lax.Precision.H...  11.8 us
  transfers between devices with their start and end apart: 5, of which 3 were waited for; matrix products, arithmetic and copies ran while one was open for 22% of the time, Pallas kernels for 0%

profile of v1, /device:TPU:1, one launch (start us, length us, event | category | flops | bytes accessed | tf_op | source)
XLA Modules:
  0.0 427.7 jit_solution(13047888640361887224)
XLA Ops:
  6.5 0.0 all-gather.11.cloned.1.call-start
  7.2 2.2 multiply_multiply_fusion.1
  9.4 0.0 copy-start.1
  9.5 0.0 copy-start.5
  9.5 3.5 copy.85
  13.0 0.0 copy-done.1
  13.0 1.6 slice_bitcast_fusion
  14.6 1.7 slice_bitcast_fusion.19
  16.3 1.7 slice_bitcast_fusion.38
  18.0 1.6 slice_bitcast_fusion.57
  19.6 9.6 %stack.259 = f32[64,1,320,1,20]{2,0,4,3,1:T(8,128)} concatenate(f32[1,1,320,1,20]{2,0,4,3,1:T(1,128)} %get-tuple-element.70, f32[1,1,320,1,20]{2,0,4,3,1:T(1,128)} %get-tuple-element.69, f32[1,1,320,1,20]{2,0,4,3,1:T(1,128)} %get-tuple-element.68, f32[1,1,320,1,20]{2,0,4,3,1:T(1,128)} %get-tuple-element.67, f32[1,1,320,1,20]{2,0,4,3,1:T(1,128)} %get-tuple-element.66, ...), dimensions={0} | concatenate | bytes 3276800 | tf_op jit(solution)/shard_map/stack | solution.py:32
  29.2 2.7 copy.86
  31.9 71.3 %all_to_all.15 = f32[64,1,320,1,20]{2,4,3,1,0:T(8,128)} all-to-all(f32[64,1,320,1,20]{2,4,3,1,0:T(8,128)S(1)} %copy.86), channel_id=1, replica_groups=mesh['chan'=64,'row'=4] {'chan'}, dimensions={0} | all-to-all | bytes 3276800 | tf_op jit(solution)/shard_map/all_to_all | solution.py:31
  103.2 2.7 reshape.162
  105.8 11.5 %fusion = f32[320,1280]{1,0:T(8,128)} fusion(f32[320,1280]{0,1:T(8,128)} %reshape.162, f32[1,1280,1280]{2,1,0:T(8,128)} %param.8), kind=kOutput, calls=%fused_computation | convolution fusion | flops 6291456000 | bytes 9830400 | tf_op jit(solution)/shard_map/cij,cjk->cik/dot_general | solution.py:8
  117.3 0.0 all-gather.11.cloned.1.call-update
  117.3 0.0 all-gather.13.cloned.1.call-start
  117.4 0.0 copy-done.5
  117.4 3.2 copy.84
  120.6 52.5 %all_to_all.16 = f32[1,320,64,20]{1,0,3,2:T(1,128)} all-to-all(f32[1,320,64,20]{1,0,3,2:T(1,128)} %bitcast.177), channel_id=1, replica_groups=mesh['chan'=64,'row'=4] {'chan'}, dimensions={2} | all-to-all | bytes 3276800 | tf_op jit(solution)/shard_map/all_to_all | solution.py:27
  173.1 7.8 %reduce.2 = f32[320,64,20]{0,2,1:T(8,128)} reduce(f32[1,320,64,20]{1,0,3,2:T(1,128)} %all_to_all.16, f32[]{:T(128)} %constant.18), dimensions={0}, to_apply=%all_to_all.9.reduce_sub_computation | reduce | bytes 3276804 | tf_op jit(solution)/shard_map/all_to_all | solution.py:27
  180.8 2.9 reshape.158
  183.8 11.5 %fusion.2 = f32[320,1280]{1,0:T(8,128)} fusion(f32[320,1280]{0,1:T(8,128)} %reshape.158, f32[1,1280,1280]{2,1,0:T(8,128)} %param.8), kind=kOutput, calls=%fused_computation.2 | convolution fusion | flops 6291456000 | bytes 9830400 | tf_op jit(solution)/shard_map/cij,cjk->cik/dot_general | solution.py:8
  195.3 0.0 all-gather.13.cloned.1.call-update
  195.3 0.0 all-gather.9.cloned.1.call-start
  195.3 0.7 all-gather.9.cloned.1.call-update
  196.0 0.0 all-gather.7.cloned.1.call-start
  196.1 0.5 all-gather.7.cloned.1.call-update
  196.6 0.0 copy-start.7
  196.6 0.0 copy-start.8
  196.6 8.5 %dot_general.37 = f32[64,20,1280]{2,1,0:T(8,128)} reshape(f32[1,1280,1280]{2,1,0:T(8,128)} %param.8) | data formatting | bytes 13107200 | tf_op jit(solution)/shard_map/cij,ckj->cik/dot_general | solution.py:50
  205.2 0.0 all-gather.11.cloned.1.call-done
  205.2 0.0 copy-start.3
  205.2 11.6 %fusion.26 = f32[320,1280]{1,0:T(8,128)} fusion(f32[1280,1280]{1,0:T(8,128)} %all-gather.11.cloned.1.call-done, f32[320,1280]{1,0:T(8,128)S(1)} %copy-done.4, f32[1280]{0:T(1024)S(1)} %get-tuple-element.6), kind=kOutput, calls=%fused_computation.21 | convolution fusion | flops 6291865600 | bytes 9835520 | tf_op jit(solution)/shard_map/cij,cjk->cik/dot_general | solution.py:8
  216.8 46.5 %all-gather.13.cloned.1.call-done = f32[1280,1280]{1,0:T(8,128)} async-done(((f32[320,1280]{1,0:T(8,128)}), f32[1280,1280]{1,0:T(8,128)}) %all-gather.13.cloned.1.call-update) | async-done | bytes 6553616 | tf_op jit(solution)/shard_map/all_gather | solution.py:43
  263.4 0.0 copy-done.3
  263.4 10.5 %fusion.19 = f32[320,1280,1]{1,0,2:T(8,128)S(1)} fusion(f32[320,1280]{1,0:T(8,128)} %fusion.26, f32[1280,1280]{1,0:T(8,128)} %all-gather.13.cloned.1.call-done, f32[320,1280]{1,0:T(8,128)S(1)} %copy-done.3, f32[1280]{0:T(1024)S(1)} %get-tuple-element.6), kind=kOutput, calls=%fused_computation.14 | convolution fusion | flops 6292275200 | bytes 11473920 | tf_op jit(solution)/shard_map/cij,cjk->cik/dot_general | solution.py:8
  273.9 11.5 %fusion.30 = f32[1,320,64,20]{1,2,3,0:T(8,128)S(1)} fusion(f32[320,1280,1]{1,0,2:T(8,128)S(1)} %fusion.19, f32[64,20,1280]{2,1,0:T(8,128)S(1)} %copy-done), kind=kOutput, calls=%fused_computation.25 | convolution fusion | flops 6291456000 | bytes 9830400 | tf_op jit(solution)/shard_map/cij,ckj->cik/dot_general | solution.py:50
  285.4 3.3 copy.88
  288.8 11.0 %all-to-all-start.2 = ((f32[1,320,64,20]{1,0,3,2:T(1,128)}), f32[1,320,64,20]{1,0,3,2:T(1,128)}, u32[]{:S(2)}, u32[]{:S(2)}) async-start(f32[1,320,64,20]{1,0,3,2:T(1,128)} %copy.88), calls=%async_computation.2 | async-start | bytes 3932160 | tf_op jit(solution)/shard_map/all_to_all | solution.py:51
  299.8 36.5 %all-gather.9.cloned.1.call-done = f32[1,1280,1280]{2,1,0:T(8,128)} async-done(((f32[1,320,1280]{2,1,0:T(8,128)}), f32[1,1280,1280]{2,1,0:T(8,128)}) %all-gather.9.cloned.1.call-update) | async-done | bytes 6553616 | tf_op jit(solution)/shard_map/all_gather | solution.py:56
  336.4 10.9 %fusion.4 = f32[320,1280]{1,0:T(8,128)} fusion(f32[1,1280,1280]{2,1,0:T(8,128)} %all-gather.9.cloned.1.call-done, f32[1,320,1280]{2,1,0:T(8,128)S(1)} %copy-done.2, f32[1280]{0:T(1024)S(1)} %get-tuple-element.5), kind=kOutput, calls=%fused_computation.4 | convolution fusion | flops 6291865600 | bytes 9835520 | tf_op jit(solution)/shard_map/cij,cjk->cik/dot_general | solution.py:8
  347.2 0.0 all-to-all-done.2
  347.3 7.8 %reduce.4 = f32[320,64,20]{0,2,1:T(8,128)} reduce(f32[1,320,64,20]{1,0,3,2:T(1,128)} %all-to-all-done.2, f32[]{:T(128)} %constant.18), dimensions={0}, to_apply=%all_to_all.11.reduce_sub_computation | reduce | bytes 3276804 | tf_op jit(solution)/shard_map/all_to_all | solution.py:51
  355.0 2.8 reshape.165
  357.9 2.2 copy.89
  360.1 49.1 %all-gather.7.cloned.1.call-done = f32[1,1280,1280]{2,1,0:T(8,128)} async-done(((f32[1,320,1280]{2,1,0:T(8,128)}), f32[1,1280,1280]{2,1,0:T(8,128)}) %all-gather.7.cloned.1.call-update) | async-done | bytes 6553616 | tf_op jit(solution)/shard_map/all_gather | solution.py:57
  409.2 11.5 %fusion.20 = f32[1,320,1280]{2,1,0:T(8,128)} fusion(f32[320,1280]{1,0:T(8,128)S(1)} %copy.89, f32[320,1280]{1,0:T(8,128)} %fusion.4, f32[1,1280,1280]{2,1,0:T(8,128)} %all-gather.7.cloned.1.call-done, f32[1280]{0:T(1024)S(1)} %fusion.37, f32[320]{0:T(512)S(1)} %fusion.38, f32[1280]{0:T(1024)S(1)} %get-tuple-element.5, f32[1,320,1280]{2,1,0:T(8,128)S(1)} %copy-done.6), kind=kOutput, calls=%fused_computation.15 | convolution fusion | flops 6294323200 | bytes 13118720 | tf_op jit(solution)/shard_map/cij,cjk->cik/dot_general | solution.py:8
  (13 shorter events, 0.1 us)
Async XLA Ops:
  6.5 198.6 %all-gather.11.cloned.1.call-start = ((), (), s32[]{:S(2)}) async-start(), calls=%async_computation.5 | async-start | bytes 8192000 | tf_op jit(solution)/shard_map/all_gather | solution.py:44
  9.4 3.5 copy-start.1
  9.5 107.9 %copy-start.5 = (f32[1,320,1280]{2,1,0:T(8,128)}, f32[1,320,1280]{2,1,0:T(8,128)S(1)}, u32[]{:S(2)}) copy-start(f32[1,320,1280]{2,1,0:T(8,128)S(1)} %get-tuple-element.71) | copy-start | bytes 4915204
  117.3 146.0 %all-gather.13.cloned.1.call-start = ((), (), s32[]{:S(2)}) async-start(), calls=%async_computation.6 | async-start | bytes 8192000 | tf_op jit(solution)/shard_map/all_gather | solution.py:43
  195.3 141.1 %all-gather.9.cloned.1.call-start = ((), (), s32[]{:S(2)}) async-start(), calls=%async_computation.4 | async-start | bytes 8192000 | tf_op jit(solution)/shard_map/all_gather | solution.py:56
  196.0 213.2 %all-gather.7.cloned.1.call-start = ((), (), s32[]{:S(2)}) async-start(), calls=%async_computation.3 | async-start | bytes 8192000 | tf_op jit(solution)/shard_map/all_gather | solution.py:57
  196.6 8.5 %copy-start.7 = (s32[1,1280]{1,0:T(1,128)S(1)}, s32[1,1280]{1,0:T(1,128)}, u32[]{:S(2)}) copy-start(s32[1,1280]{1,0:T(1,128)} %param.11) | copy-start | bytes 15364
  196.6 8.5 %copy-start.8 = (s32[1,1280]{1,0:T(1,128)S(1)}, s32[1,1280]{1,0:T(1,128)}, u32[]{:S(2)}) copy-start(s32[1,1280]{1,0:T(1,128)} %param.10) | copy-start | bytes 15364
  196.6 8.6 %copy-start.4 = (f32[320,1280]{1,0:T(8,128)S(1)}, f32[320,1280]{1,0:T(8,128)}, u32[]{:S(2)}) copy-start(f32[320,1280]{1,0:T(8,128)} %fusion.2) | copy-start | bytes 4915204
  205.2 58.2 %copy-start.3 = (f32[320,1280]{1,0:T(8,128)S(1)}, f32[320,1280]{1,0:T(8,128)}, u32[]{:S(2)}) copy-start(f32[320,1280]{1,0:T(8,128)} %fusion) | copy-start | bytes 4915204
  263.4 10.5 %copy-start = (f32[64,20,1280]{2,1,0:T(8,128)S(1)}, f32[64,20,1280]{2,1,0:T(8,128)}, u32[]{:S(2)}) copy-start(f32[64,20,1280]{2,1,0:T(8,128)} %dot_general.37) | copy-start | bytes 19660804
  288.8 47.6 %copy-start.2 = (f32[1,320,1280]{2,1,0:T(8,128)S(1)}, f32[1,320,1280]{2,1,0:T(8,128)}, u32[]{:S(2)}) copy-start(f32[1,320,1280]{2,1,0:T(8,128)} %copy-done.1) | copy-start | bytes 4915204
  288.8 58.5 %all-to-all-start.2 = ((f32[1,320,64,20]{1,0,3,2:T(1,128)}), f32[1,320,64,20]{1,0,3,2:T(1,128)}, u32[]{:S(2)}, u32[]{:S(2)}) async-start(f32[1,320,64,20]{1,0,3,2:T(1,128)} %copy.88), calls=%async_computation.2 | async-start | bytes 3932160 | tf_op jit(solution)/shard_map/all_to_all | solution.py:51
  357.9 51.3 %copy-start.6 = (f32[1,320,1280]{2,1,0:T(8,128)S(1)}, f32[1,320,1280]{2,1,0:T(8,128)}, u32[]{:S(2)}) copy-start(f32[1,320,1280]{2,1,0:T(8,128)} %param.6) | copy-start | bytes 4915204
Sparse Core Ops, SparseCore 0:
  117.4 65.7 all-gather.10
  195.4 67.9 all-gather.12
  265.2 71.1 all-gather.8
  338.0 71.1 all-gather.6
